TPU v7x, 128 devices: a whole 4x4x4 slice. The times are simulated.
128 devices in a mesh: dp: 2 (over z_lo), seq: 64 (over x, z_hi, y, core).
Axes of the slice: x: 4, y: 4, z: 4 (z_hi: 2, z_lo: 2; z = z_hi * 2 + z_lo), core: 2. Of those that a mesh axis runs over, the one named last changes fastest.
Arguments:
- query_raw: bfloat16 [2, 131072, 768], P('dp', 'seq'), may hold values from -6 to 6
- key_raw: bfloat16 [2, 131072, 768], P('dp', 'seq'), may hold values from -6 to 6
- value_raw: bfloat16 [2, 131072, 768], P('dp', 'seq'), may hold values from -6 to 6
- out_grad: bfloat16 [2, 131072, 768], P('dp', 'seq'), may hold values from -6 to 6
- conv_taps: float32 [3, 3, 768], replicated, may hold values from -3 to 3
- left_block: bfloat16 [512, 512], replicated, may hold values from -0.25 to 0.25
- right_block: bfloat16 [256, 256], replicated, may hold values from -0.375 to 0.375
- twiddle: float32 [256, 512], P('seq'), may hold values from 0.5 to 2
Outputs:
- query_grad: bfloat16 [2, 131072, 768], P('dp', 'seq')
- key_grad: bfloat16 [2, 131072, 768], P('dp', 'seq')
- value_grad: bfloat16 [2, 131072, 768], P('dp', 'seq')
- conv_grad: float32 [3, 3, 768], replicated
- left_grad: float32 [512, 512], replicated
- right_grad: float32 [256, 256], replicated
- twiddle_grad: float32 [256, 512], P('seq')
All inputs are finite; a program needn't handle non-finite values.
Results may differ from a plain program's by a relative error of at most 0.0064.
Values may be sent and summed in bfloat16 or wider, within the bound.
A program may use at most 192 MiB of HBM per device.

v0:
```python
import jax
import jax.numpy as jnp
from jax import lax
from jax.sharding import PartitionSpec as P


def shifted(value, axis, steps):
    count = lax.axis_size(axis)
    initial, last = (max(0, -steps), min(count, count - steps))
    return lax.ppermute(value, axis, [(source, source + steps) for source in range(initial, last)])


def short_conv(padded, tap_rows):
    return (
        tap_rows[0] * padded[:, 2:] + tap_rows[1] * padded[:, 1:-1] + tap_rows[2] * padded[:, :-2]
    )


def conv_back(grads, after, tap_rows):
    extended = jnp.concatenate([grads, after], 1)
    return (
        tap_rows[0] * extended[:, :-2]
        + tap_rows[1] * extended[:, 1:-1]
        + tap_rows[2] * extended[:, 2:]
    )


def tap_terms(grads, padded):
    return jnp.stack(
        [
            jnp.sum(grads * padded[:, 2:], (0, 1)),
            jnp.sum(grads * padded[:, 1:-1], (0, 1)),
            jnp.sum(grads * padded[:, :-2], (0, 1)),
        ]
    )


def shards(query_raw, key_raw, value_raw, out_grad, conv_taps, left_block, right_block, twiddle):
    batch_here, tokens_here, channels = query_raw.shape
    columns = left_block.shape[0]
    rows_here = tokens_here // columns
    block_shape = (batch_here, rows_here, columns, channels)
    prior = shifted((query_raw[:, -2:], key_raw[:, -2:], value_raw[:, -2:]), "seq", 1)
    raws = (query_raw, key_raw, value_raw)
    padded_all = [
        jnp.concatenate([prior[stream].astype(jnp.float32), raws[stream].astype(jnp.float32)], 1)
        for stream in range(3)
    ]
    q_conv = short_conv(padded_all[0], conv_taps[0])
    k_conv = short_conv(padded_all[1], conv_taps[1])
    v_conv = short_conv(padded_all[2], conv_taps[2])
    gated = (k_conv * v_conv).astype(jnp.bfloat16).reshape(block_shape)
    mixed = jnp.einsum("bd,nadc->nabc", left_block, gated, preferred_element_type=jnp.float32)
    twist = twiddle[None, :, :, None]
    scaled = (mixed * twist).astype(jnp.bfloat16)
    upstream = out_grad.astype(jnp.float32).reshape(block_shape)
    gate_grad = (upstream * q_conv.reshape(block_shape)).astype(jnp.bfloat16)
    pieces = lax.all_to_all(scaled, "seq", split_axis=2, concat_axis=1, tiled=True)
    monarch_cols = jnp.einsum(
        "ae,nebc->nabc", right_block, pieces, preferred_element_type=jnp.float32
    ).astype(jnp.bfloat16)
    monarch = lax.all_to_all(monarch_cols, "seq", split_axis=1, concat_axis=2, tiled=True)
    gate_cols = lax.all_to_all(gate_grad, "seq", split_axis=2, concat_axis=1, tiled=True)
    scaled_grad_cols = jnp.einsum(
        "ae,nabc->nebc", right_block, gate_cols, preferred_element_type=jnp.float32
    ).astype(jnp.bfloat16)
    right_part = jnp.einsum("nabc,nebc->ae", gate_cols, pieces, preferred_element_type=jnp.float32)
    scaled_grad = lax.all_to_all(scaled_grad_cols, "seq", split_axis=1, concat_axis=2, tiled=True)
    q_conv_grad = (upstream * monarch.astype(jnp.float32)).reshape(
        batch_here, tokens_here, channels
    )
    scaled_wide = scaled_grad.astype(jnp.float32)
    twist_part = jnp.sum(scaled_wide * mixed, axis=(0, 3))
    twist_total = lax.psum(twist_part, "dp")
    mixed_grad = (scaled_wide * twist).astype(jnp.bfloat16)
    gated_grad = jnp.einsum(
        "bd,nabc->nadc", left_block, mixed_grad, preferred_element_type=jnp.float32
    ).reshape(batch_here, tokens_here, channels)
    left_part = jnp.einsum("nabc,nadc->bd", mixed_grad, gated, preferred_element_type=jnp.float32)
    grads = (q_conv_grad, gated_grad * v_conv, gated_grad * k_conv)
    after = shifted((grads[0][:, :2], grads[1][:, :2], grads[2][:, :2]), "seq", -1)
    outputs = [
        conv_back(grads[stream], after[stream], conv_taps[stream]).astype(jnp.bfloat16)
        for stream in range(3)
    ]
    tap_part = jnp.stack([tap_terms(grads[stream], padded_all[stream]) for stream in range(3)])
    left_total, right_total, tap_total = lax.psum((left_part, right_part, tap_part), ("dp", "seq"))
    return (outputs[0], outputs[1], outputs[2], tap_total, left_total, right_total, twist_total)


def solution(mesh):
    placed = (
        P("dp", "seq", None),
        P("dp", "seq", None),
        P("dp", "seq", None),
        P("dp", "seq", None),
        P(),
        P(),
        P(),
        P("seq", None),
    )
    return jax.shard_map(
        shards,
        mesh=mesh,
        in_specs=placed,
        out_specs=(
            P("dp", "seq", None),
            P("dp", "seq", None),
            P("dp", "seq", None),
            P(),
            P(),
            P(),
            P("seq", None),
        ),
        check_vma=False,
    )
```

profile of v0, /device:TPU:1, one launch (start us, length us, event | category | flops | bytes accessed | tf_op | source)
XLA Modules:
  0.0 479.2 jit_solution(6440206345614049939)
XLA Ops:
  7.2 0.9 slice.138
  8.1 4.7 collective-permute-start.3
  12.8 0.9 slice_reduce_fusion.8
  13.7 2.4 convert_element_type.153
  16.2 2.6 fusion.18
  18.8 2.4 copy.63
  21.3 52.3 %all_to_all.48 = bf16[1,4,512,768]{3,1,0,2:T(4,128)(2,1)S(1)} all-to-all(bf16[1,4,512,768]{3,1,0,2:T(4,128)(2,1)S(1)} %copy.63), channel_id=1, replica_groups=mesh['dp'=2,'seq'=64] {'seq'}, dimensions={2} | all-to-all | bytes 6291456 | tf_op jit(solution)/shard_map/all_to_all | solution.py:63
  73.6 0.4 copy.107
  74.0 0.4 copy.65
  74.4 1.7 copy-done.13
  76.1 3.0 convert_bitcast_fusion.2
  79.1 5.0 %copy.67 = bf16[1,256,8,768]{3,2,0,1:T(8,128)(2,1)} copy(bf16[1,256,8,768]{1,3,2,0:T(8,128)(2,1)} %convert_bitcast_fusion.2) | data formatting | bytes 6291456 | tf_op jit(solution)/shard_map/convert_element_type | solution.py:66
  84.0 5.3 %all-to-all-start.3 = ((bf16[1,256,8,768]{3,2,0,1:T(8,128)(2,1)}), bf16[1,256,8,768]{3,2,0,1:T(8,128)(2,1)}, u32[]{:S(2)}, u32[]{:S(2)}) async-start(bf16[1,256,8,768]{3,2,0,1:T(8,128)(2,1)} %copy.67), calls=%async_computation.3 | async-start | bytes 6291456 | tf_op jit(solution)/shard_map/all_to_all | solution.py:68
  89.3 0.9 slice.123
  90.2 3.7 collective-permute-start
  93.9 0.7 slice.129
  94.6 2.2 collective-permute-start.1
  96.8 5.1 %convert_element_type.139 = f32[1,2048,768]{2,1,0:T(8,128)} convert(bf16[1,2048,768]{2,1,0:T(8,128)(2,1)} %param.9) | non-fusion elementwise | flops 1572864 | bytes 9437184 | tf_op jit(solution)/shard_map/convert_element_type | solution.py:46
  101.9 3.2 convert_element_type.141
  105.1 10.8 %collective-permute-done = bf16[1,2,768]{2,1,0:T(2,128)(2,1)S(1)} collective-permute-done((bf16[1,2,768]{2,1,0:T(2,128)(2,1)S(1)}, bf16[1,2,768]{2,1,0:T(2,128)(2,1)S(1)}, u32[]{:S(2)}, u32[]{:S(2)}) %collective-permute-start) | collective-permute-done | bytes 3104 | tf_op jit(solution)/shard_map/ppermute | solution.py:10
  116.0 0.2 collective-permute-done.1
  116.2 15.0 %all-to-all-done.3 = bf16[1,256,8,768]{3,2,0,1:T(8,128)(2,1)} async-done(((bf16[1,256,8,768]{3,2,0,1:T(8,128)(2,1)}), bf16[1,256,8,768]{3,2,0,1:T(8,128)(2,1)}, u32[]{:S(2)}, u32[]{:S(2)}) %all-to-all-start.3) | async-done | bytes 3145760 | tf_op jit(solution)/shard_map/all_to_all | solution.py:68
  131.2 4.2 fusion.25
  135.5 13.2 %multiply_reduce_fusion.1 = (f32[768]{0:T(1024)S(1)}, f32[768]{0:T(1024)S(1)}, f32[768]{0:T(1024)S(1)}, f32[1,2048,768]{2,1,0:T(8,128)S(1)}, f32[1,2048,768]{2,1,0:T(8,128)}) fusion(f32[1,2048,768]{2,1,0:T(8,128)} %convert_element_type.141, f32[1,2,768]{2,1,0:T(2,128)S(1)} %convert_element_type.142, bf16[1,2048,768]{2,1,0:T(8,128)(2,1)} %param.10, ...), kind=kLoop, calls=%fused_computation.54 | loop fusion | flops 26736384 | bytes 34633728 | tf_op jit(solution)/shard_map/reduce_sum | solution.py:32
  148.7 2.6 copy-done.3
  151.3 2.4 collective-permute-start.5
  153.7 5.1 %copy_bitcast_fusion = f32[1,4,512,768]{3,2,1,0:T(8,128)} fusion(bf16[1,64,4,8,768]{4,3,2,1,0:T(8,128)(2,1)} %bitcast.33), kind=kLoop, calls=%fused_computation.65 | loop fusion | flops 1572864 | bytes 9437184 | tf_op jit(solution)/shard_map/convert_element_type | solution.py:72
  158.8 6.6 %copy.76 = f32[1,4,512,768]{2,3,1,0:T(8,128)} copy(f32[1,4,512,768]{3,2,1,0:T(8,128)} %copy_bitcast_fusion) | data formatting | bytes 12582912 | tf_op jit(solution)/shard_map/convert_element_type | solution.py:72
  165.4 25.6 %multiply_reduce_fusion.4 = (f32[768]{0:T(1024)S(1)}, f32[768]{0:T(1024)S(1)}, f32[768]{0:T(1024)S(1)}, f32[1,2048,768]{2,1,0:T(8,128)}, f32[1,2048,768]{2,1,0:T(8,128)}, /*index=5*/bf16[1,2048,768]{2,1,0:T(8,128)(2,1)}) fusion(f32[1,2048,768]{2,1,0:T(8,128)} %convert_element_type.139, f32[1,2,768]{2,1,0:T(2,128)S(1)} %convert_element_type.140, ...), kind=kLoop, calls=%fused_computation.57 | loop fusion | flops 39319296 | bytes 44077056 | tf_op jit(solution)/shard_map/reduce_sum | solution.py:32
  191.0 5.4 %multiply_convert_fusion.1 = bf16[1,2048,768]{2,1,0:T(8,128)(2,1)S(1)} fusion(f32[1,2048,768]{2,1,0:T(8,128)} %get-tuple-element.31, f32[1,2048,768]{2,1,0:T(8,128)} %get-tuple-element.29), kind=kLoop, calls=%fused_computation.62 | loop fusion | flops 3145728 | bytes 15728640 | tf_op jit(solution)/shard_map/convert_element_type | solution.py:52
  196.4 1.0 copy-done.4
  197.4 3.9 fusion.23
  201.3 6.0 %copy.56 = bf16[1,4,512,768]{3,1,0,2:T(4,128)(2,1)} copy(bf16[1,4,512,768]{2,3,1,0:T(8,128)(2,1)} %get-tuple-element.33) | data formatting | bytes 6291456 | tf_op jit(solution)/shard_map/convert_element_type | solution.py:55
  207.2 48.1 %all_to_all.49 = bf16[1,4,512,768]{3,1,0,2:T(4,128)(2,1)S(1)} all-to-all(bf16[1,4,512,768]{3,1,0,2:T(4,128)(2,1)} %copy.56), channel_id=1, replica_groups=mesh['dp'=2,'seq'=64] {'seq'}, dimensions={2} | all-to-all | bytes 6291456 | tf_op jit(solution)/shard_map/all_to_all | solution.py:58
  255.3 0.4 copy.108
  255.7 0.4 copy.58
  256.1 1.7 copy-done.8
  257.8 3.0 convert_bitcast_fusion.3
  260.8 5.0 %copy.60 = bf16[1,256,8,768]{3,2,0,1:T(8,128)(2,1)} copy(bf16[1,256,8,768]{1,3,2,0:T(8,128)(2,1)} %convert_bitcast_fusion.3) | data formatting | bytes 6291456 | tf_op jit(solution)/shard_map/convert_element_type | solution.py:61
  265.7 5.3 %all-to-all-start.1 = ((bf16[1,256,8,768]{3,2,0,1:T(8,128)(2,1)}), bf16[1,256,8,768]{3,2,0,1:T(8,128)(2,1)}, u32[]{:S(2)}, u32[]{:S(2)}) async-start(bf16[1,256,8,768]{3,2,0,1:T(8,128)(2,1)} %copy.60), calls=%async_computation.1 | async-start | bytes 6291456 | tf_op jit(solution)/shard_map/all_to_all | solution.py:62
  271.0 0.0 all-reduce.3.cloned.1.call-start
  271.1 0.1 mul.286
  271.2 0.1 copy.71
  271.4 0.7 slice.156
  272.1 2.5 collective-permute-start.4
  274.7 5.6 %fusion.42 = f32[512,512]{1,0:T(8,128)} fusion(bf16[4,512,768]{2,1,0:T(8,128)(2,1)} %bitcast.109, f32[4,64,8]{2,0,1:T(4,128)S(1)} %copy.71, bf16[1,64,4,8,768]{4,3,2,1,0:T(8,128)(2,1)} %bitcast.33), kind=kOutput, calls=%fused_computation.82 | convolution fusion | flops 1615331328 | bytes 7348224 | tf_op jit(solution)/shard_map/nabc,nadc->bd/dot_general | solution.py:79
  280.3 20.6 %psum.31 = f32[4,512]{1,0:T(4,128)} all-reduce(f32[4,512]{1,0:T(4,128)S(1)} %get-tuple-element.32), channel_id=1, replica_groups=mesh['dp'=2,'seq'=64] {'dp'}, use_global_device_ids=true, to_apply=%region_13.0 | all-reduce | flops 2048 | bytes 16384 | tf_op jit(solution)/shard_map/psum | solution.py:74
  300.9 4.6 collective-permute-done.4
  305.5 9.2 %fusion.9 = bf16[1,2048,768]{2,1,0:T(8,128)(2,1)} fusion(f32[1,2048,768]{2,1,0:T(8,128)} %get-tuple-element.28, f32[1,2,768]{2,1,0:T(2,128)S(1)} %collective-permute-done.4, f32[768]{0:T(1024)S(1)} %get-tuple-element.20, f32[768]{0:T(1024)S(1)} %get-tuple-element.21, f32[768]{0:T(1024)S(1)} %get-tuple-element.22), kind=kLoop, calls=%fused_computation.23 | loop fusion | flops 12582912 | bytes 9452544 | tf_op jit(solution)/shard_map/convert_element_type | solution.py:83
  314.6 2.5 fusion.45
  317.1 0.0 all-reduce.3.cloned.1.call-update
  317.1 2.9 convert_bitcast_fusion
  320.1 0.6 copy.62
  320.7 1.0 slice-done.1
  321.7 0.9 copy-done.6
  322.6 0.9 copy-done.11
  323.5 3.6 multiply_reduce_fusion.7
  327.1 2.6 copy-done.2
  329.7 1.9 collective-permute-start.2
  331.7 70.2 %psum.28 = f32[3,3,768]{2,1,0:T(4,128)} all-reduce(f32[3,3,768]{2,1,0:T(4,128)S(1)} %pad_maximum_fusion.6), channel_id=1, replica_groups=mesh['dp'=2,'seq'=64] {'dp','seq'}, use_global_device_ids=true, to_apply=%region_9.0 | all-reduce | flops 6912 | bytes 55296 | tf_op jit(solution)/shard_map/psum | solution.py:87
  401.8 9.0 %fusion.15 = bf16[1,2048,768]{2,1,0:T(8,128)(2,1)} fusion(f32[1,2048,768]{2,1,0:T(8,128)} %copy-done.2, f32[1,2,768]{2,1,0:T(2,128)S(1)} %collective-permute-done.2, f32[768]{0:T(1024)S(1)} %get-tuple-element.23, f32[768]{0:T(1024)S(1)} %get-tuple-element.24, f32[768]{0:T(1024)S(1)} %get-tuple-element.16), kind=kLoop, calls=%fused_computation.29 | loop fusion | flops 12582912 | bytes 9452544 | tf_op jit(solution)/shard_map/convert_element_type | solution.py:83
  410.9 57.6 %all-reduce.3.cloned.1.call-done = (f32[512,512]{1,0:T(8,128)}, f32[256,256]{1,0:T(8,128)}) async-done(((f32[512,512]{1,0:T(8,128)}, f32[256,256]{1,0:T(8,128)}), (f32[512,512]{1,0:T(8,128)}, f32[256,256]{1,0:T(8,128)})) %all-reduce.3.cloned.1.call-update) | async-done | bytes 1310736 | tf_op jit(solution)/shard_map/psum | solution.py:87
  468.5 2.3 copy.111
  470.7 1.7 copy.112
  (57 shorter events, 0.2 us)
Async XLA Ops:
  7.2 124.0 %copy-start = (bf16[512,512]{1,0:T(8,128)(2,1)S(1)}, bf16[512,512]{1,0:T(8,128)(2,1)}, u32[]{:S(2)}) copy-start(bf16[512,512]{1,0:T(8,128)(2,1)} %param.13) | copy-start | bytes 1572868
  7.2 9.0 %copy-start.10 = (bf16[1,2048,768]{2,1,0:T(8,128)(2,1)S(1)}, bf16[1,2048,768]{2,1,0:T(8,128)(2,1)}, u32[]{:S(2)}) copy-start(bf16[1,2048,768]{2,1,0:T(8,128)(2,1)} %param.11) | copy-start | bytes 9437188
  8.1 8.1 %collective-permute-start.3 = (bf16[1,2,768]{2,1,0:T(2,128)(2,1)S(1)}, bf16[1,2,768]{2,1,0:T(2,128)(2,1)S(1)}, u32[]{:S(2)}, u32[]{:S(2)}) collective-permute-start(bf16[1,2,768]{2,1,0:T(2,128)(2,1)S(1)} %slice.138), channel_id=1, source_target_pairs={{0,1},{1,2},{2,3},{3,4},{4,5},{5,6},{6,7},{7,8},{8,9},{9,10},{10,1... | collective-permute-start | bytes 9224 | tf_op jit(solution)/shard_map/ppermute | solution.py:10
  16.1 2.7 copy-start.1
  73.6 2.5 copy-start.15
  74.4 1.7 copy-start.13
  84.0 47.1 %all-to-all-start.3 = ((bf16[1,256,8,768]{3,2,0,1:T(8,128)(2,1)}), bf16[1,256,8,768]{3,2,0,1:T(8,128)(2,1)}, u32[]{:S(2)}, u32[]{:S(2)}) async-start(bf16[1,256,8,768]{3,2,0,1:T(8,128)(2,1)} %copy.67), calls=%async_computation.3 | async-start | bytes 6291456 | tf_op jit(solution)/shard_map/all_to_all | solution.py:68
  89.3 12.6 %copy-start.7 = (bf16[1,2048,768]{2,1,0:T(8,128)(2,1)S(1)}, bf16[1,2048,768]{2,1,0:T(8,128)(2,1)}, u32[]{:S(2)}) copy-start(bf16[1,2048,768]{2,1,0:T(8,128)(2,1)} %param.10) | copy-start | bytes 9437188
  90.2 25.7 %collective-permute-start = (bf16[1,2,768]{2,1,0:T(2,128)(2,1)S(1)}, bf16[1,2,768]{2,1,0:T(2,128)(2,1)S(1)}, u32[]{:S(2)}, u32[]{:S(2)}) collective-permute-start(bf16[1,2,768]{2,1,0:T(2,128)(2,1)S(1)} %slice.123), channel_id=1, source_target_pairs={{0,1},{1,2},{2,3},{3,4},{4,5},{5,6},{6,7},{7,8},{8,9},{9,10},{10,1... | collective-permute-start | bytes 9224 | tf_op jit(solution)/shard_map/ppermute | solution.py:10
  94.6 21.6 %collective-permute-start.1 = (bf16[1,2,768]{2,1,0:T(2,128)(2,1)S(1)}, bf16[1,2,768]{2,1,0:T(2,128)(2,1)S(1)}, u32[]{:S(2)}, u32[]{:S(2)}) collective-permute-start(bf16[1,2,768]{2,1,0:T(2,128)(2,1)S(1)} %slice.129), channel_id=1, source_target_pairs={{0,1},{1,2},{2,3},{3,4},{4,5},{5,6},{6,7},{7,8},{8,9},{9,10},{10,1... | collective-permute-start | bytes 9224 | tf_op jit(solution)/shard_map/ppermute | solution.py:10
  101.9 29.3 %copy-start.16 = (f32[4,512]{1,0:T(4,128)S(1)}, f32[4,512]{1,0:T(4,128)}, u32[]{:S(2)}) copy-start(f32[4,512]{1,0:T(4,128)} %param.15) | copy-start | bytes 24580
  101.9 33.5 %slice-start.2 = ((s8[6291456]{0:T(1024)(128)(4,1)}), s8[2097152]{0:T(1024)(128)(4,1)S(1)}, s32[]{:S(2)}) async-start(s8[6291456]{0:T(1024)(128)(4,1)} %bitcast.101), calls=%async_computation.7 | async-start | bytes 4194304
  131.2 4.3 slice-start.3
  135.5 13.3 %copy-start.5 = (f32[4,768,512]{1,2,0:T(8,128)}, f32[4,768,512]{1,2,0:T(8,128)S(1)}, u32[]{:S(2)}) copy-start(f32[4,768,512]{1,2,0:T(8,128)S(1)} %fusion.25) | copy-start | bytes 18874372
  148.7 2.6 copy-start.3
  151.3 14.1 %collective-permute-start.5 = (f32[1,2,768]{2,1,0:T(2,128)S(1)}, f32[1,2,768]{2,1,0:T(2,128)S(1)}, u32[]{:S(2)}, u32[]{:S(2)}) collective-permute-start(f32[1,2,768]{2,1,0:T(2,128)S(1)} %slice.159), channel_id=1, source_target_pairs={{1,0},{2,1},{3,2},{4,3},{5,4},{6,5},{7,6},{8,7},{9,8},{10,9},{11,1... | collective-permute-start | bytes 18440 | tf_op jit(solution)/shard_map/ppermute | solution.py:10
  191.0 6.4 %copy-start.4 = (f32[1,4,512,768]{2,3,1,0:T(8,128)S(1)}, f32[1,4,512,768]{2,3,1,0:T(8,128)}, u32[]{:S(2)}) copy-start(f32[1,4,512,768]{2,3,1,0:T(8,128)} %copy.76) | copy-start | bytes 18874372
  196.4 4.9 %copy-start.12 = (bf16[1,2048,768]{2,1,0:T(8,128)(2,1)}, bf16[1,2048,768]{2,1,0:T(8,128)(2,1)S(1)}, u32[]{:S(2)}) copy-start(bf16[1,2048,768]{2,1,0:T(8,128)(2,1)S(1)} %multiply_convert_fusion.1) | copy-start | bytes 9437188
  256.1 1.7 copy-start.8
  265.7 51.4 %all-to-all-start.1 = ((bf16[1,256,8,768]{3,2,0,1:T(8,128)(2,1)}), bf16[1,256,8,768]{3,2,0,1:T(8,128)(2,1)}, u32[]{:S(2)}, u32[]{:S(2)}) async-start(bf16[1,256,8,768]{3,2,0,1:T(8,128)(2,1)} %copy.60), calls=%async_computation.1 | async-start | bytes 6291456 | tf_op jit(solution)/shard_map/all_to_all | solution.py:62
  271.0 197.4 %all-reduce.3.cloned.1.call-start = ((), (), s32[]{:S(2)}) async-start(), calls=%async_computation.4 | async-start | bytes 2621440 | tf_op jit(solution)/shard_map/psum | solution.py:87
  272.1 33.4 %collective-permute-start.4 = (f32[1,2,768]{2,1,0:T(2,128)S(1)}, f32[1,2,768]{2,1,0:T(2,128)S(1)}, u32[]{:S(2)}, u32[]{:S(2)}) collective-permute-start(f32[1,2,768]{2,1,0:T(2,128)S(1)} %slice.156), channel_id=1, source_target_pairs={{1,0},{2,1},{3,2},{4,3},{5,4},{6,5},{7,6},{8,7},{9,8},{10,9},{11,1... | collective-permute-start | bytes 18440 | tf_op jit(solution)/shard_map/ppermute | solution.py:10
  300.9 13.8 %copy-start.9 = (bf16[1,64,4,8,768]{4,3,2,1,0:T(8,128)(2,1)S(1)}, bf16[1,64,4,8,768]{4,3,2,1,0:T(8,128)(2,1)}, u32[]{:S(2)}) copy-start(bf16[1,64,4,8,768]{4,3,2,1,0:T(8,128)(2,1)} %copy-done.8) | copy-start | bytes 9437188
  300.9 13.8 %copy-start.14 = (bf16[1,64,4,8,768]{4,3,2,1,0:T(8,128)(2,1)S(1)}, bf16[1,64,4,8,768]{4,3,2,1,0:T(8,128)(2,1)}, u32[]{:S(2)}) copy-start(bf16[1,64,4,8,768]{4,3,2,1,0:T(8,128)(2,1)} %copy-done.13) | copy-start | bytes 9437188
  317.1 3.5 slice-start
  320.0 1.7 slice-start.1
  320.0 2.5 copy-start.6
  320.0 3.4 copy-start.11
  327.0 2.7 copy-start.2
  329.7 72.1 %collective-permute-start.2 = (f32[1,2,768]{2,1,0:T(2,128)S(1)}, f32[1,2,768]{2,1,0:T(2,128)S(1)}, u32[]{:S(2)}, u32[]{:S(2)}) collective-permute-start(f32[1,2,768]{2,1,0:T(2,128)S(1)} %slice.151), channel_id=1, source_target_pairs={{1,0},{2,1},{3,2},{4,3},{5,4},{6,5},{7,6},{8,7},{9,8},{10,9},{11,1... | collective-permute-start | bytes 18440 | tf_op jit(solution)/shard_map/ppermute | solution.py:10
Sparse Core Ops, SparseCore 0:
  317.2 151.1 all-reduce.2
where the time goes:
time: 480 us; the launch traced here: 479 us
  blocking collectives  191 us (40%)
  waiting for transfers between devices  88.3 us (18%)
  other arithmetic  87.3 us (18%)
  local copies, waits for them, and re-layouts  47.8 us (10%)
  starting transfers between devices  28.1 us (6%)
  matrix products  22.2 us (5%)
  between operations  14.5 us (3%)
    psum x1, blocking collectives, shards(): lax.psum((left_part, right_part, tap_part), ('dp', 'seq'))  70.2 us
    psum x1, waiting for transfers between devices, shards(): lax.psum((left_part, right_part, tap_part), ('dp', 'seq'))  57.6 us
    all_to_all x1, blocking collectives, shards(): lax.all_to_all(gate_grad, 'seq', split_axis=2, concat_axis=1, tiled=True)  52.3 us
    all_to_all x1, blocking collectives, shards(): lax.all_to_all(scaled, 'seq', split_axis=2, concat_axis=1, tiled=True)  48.1 us
    reduce_sum x3, other arithmetic, tap_terms(): jnp.sum(grads * padded[:, 1:-1], (0, 1))  42.4 us
    psum x1, blocking collectives, shards(): twist_total = lax.psum(twist_part, 'dp')  20.6 us
    convert_element_type x2, other arithmetic, shards(): conv_back(grads[stream], after[stream], conv_taps[stream])  18.2 us
    ppermute x6, starting transfers between devices, shifted(): lax.ppermute(value, axis, [(source, source + steps) for source in range(i...  17.5 us
  transfers between devices with their start and end apart: 9, of which 5 were waited for; matrix products, arithmetic and copies ran while one was open for 12% of the time, Pallas kernels for 0%

commit v1 on v0

v1 whole, which is shorter than its diff:
```python
import jax
import jax.numpy as jnp
from jax import lax
from jax.experimental import pallas as pl
from jax.experimental.pallas import tpu as pltpu
from jax.sharding import PartitionSpec as P

F32, BF16 = jnp.float32, jnp.bfloat16
MESH = pl.DeviceIdType.MESH
SEQ, DP = 64, 2
DEVICES = SEQ * DP
ROWS, COLS, CH = 4, 512, 768
TOKENS = ROWS * COLS
CC = 256
NC = CH // CC
LANES = CC // 128
TILES = CH // 128
WHOLE = TOKENS + 16
VMEM_LIMIT = 62 * 2**20


def dot(a, b):
    return jnp.dot(a, b, preferred_element_type=F32)


def dot_nt(a, b):
    return lax.dot_general(a, b, (((1,), (1,)), ((), ())), preferred_element_type=F32)


def loop(lo, hi, body):
    def step(i, carry):
        body(i)
        return carry

    lax.fori_loop(lo, hi, step, 0)


def wide(column):
    return jnp.concatenate([column] * LANES, axis=1)


def kernel(
    q_in, k_in, v_in, o_in, taps, left, right, twist,
    q_out, k_out, v_out, conv_out, left_out, right_out, twist_out,
    xq, xk, xv, xo, gs, gr, br, ss, sr, mr, gd, gated, sd, zb, mg, gk, gv,
    obuf, mh, kh, perm, perm_t, left_t, right_t, twist_t, twist_acc, tws, twx,
    left_acc, right_acc, lx, lb, li, lsum, lg, lg2, rb, ri, rsum, rg,
    ckv, cq, ci, cj, csum, cg,
    in_sem, halo_s, halo_r, a2a_s, a2a_r, mh_s, mh_r, kh_s, kh_r, out_sem,
    l_s, l_r, r_s, r_r, c_s, c_r, tw_s, tw_r,
):
    d, s = lax.axis_index("dp"), lax.axis_index("seq")
    x, zh, y, core = s // 16, (s // 8) % 2, (s // 2) % 4, s % 2
    me = d * SEQ + s
    chip = d * 32 + s // 2
    first, last = s == 0, s == SEQ - 1

    def peer(i):
        o = (i * 9) % 64
        bit = [(o // (1 << n)) % 2 for n in range(6)]
        dx, dz, dy, dc = 2 * bit[0] + bit[2], bit[1], 2 * bit[3] + bit[4], bit[5]
        dx = dx + core * (4 - 2 * dx)
        dy = dy + core * (4 - 2 * dy)
        return (((x + dx) % 4 * 2 + (zh + dz) % 2) * 4 + (y + dy) % 4) * 2 + (core + dc) % 2

    def local(src, dst, sem):
        return pltpu.make_async_copy(src, dst, sem)

    def remote(src, dst, ssem, rsem, dev):
        return pltpu.make_async_remote_copy(
            src_ref=src, dst_ref=dst, send_sem=ssem, recv_sem=rsem, device_id=dev, device_id_type=MESH
        )

    def wait_bytes(ref, sem):
        pltpu.make_async_copy(ref, ref, sem).wait()

    def lane(cc):
        return pl.ds(cc * CC, CC)

    barrier = pltpu.get_barrier_semaphore()

    def greet(i):
        t = (me + i) % DEVICES
        pl.semaphore_signal(barrier, inc=1, device_id=(t // SEQ, t % SEQ), device_id_type=MESH)

    loop(1, DEVICES, greet)

    ins = (q_in, o_in, k_in, v_in)
    bufs = (xq, xo, xk, xv)

    def load(n, cc):
        row = 0 if n == 1 else 16
        return local(ins[n].at[:, lane(cc)], bufs[n].at[cc, pl.ds(row, TOKENS)], in_sem.at[n, cc])

    for pair in ((0, 1), (2, 3)):
        for cc in range(NC):
            for n in pair:
                load(n, cc).start()

    def halo(n, cc):
        if n == 1:
            return remote(o_in.at[pl.ds(0, 16), lane(cc)], xo.at[cc, pl.ds(TOKENS, 16)],
                          halo_s.at[n, cc], halo_r.at[n, cc], (d, jnp.maximum(s - 1, 0)))
        return remote(ins[n].at[pl.ds(TOKENS - 16, 16), lane(cc)], bufs[n].at[cc, pl.ds(0, 16)],
                      halo_s.at[n, cc], halo_r.at[n, cc], (d, jnp.minimum(s + 1, SEQ - 1)))

    @pl.when(first)
    def _():
        for ref in (xq, xk, xv):
            ref[:, 0:16, :] = jnp.zeros((NC, 16, CC), BF16)

    @pl.when(last)
    def _():
        xo[:, TOKENS:WHOLE, :] = jnp.zeros((NC, 16, CC), BF16)
        mh[...] = jnp.zeros_like(mh)
        kh[...] = jnp.zeros_like(kh)

    def tap(stream, j, cc):
        return taps[stream, j : j + 1, cc * CC : (cc + 1) * CC]

    def shifts(ref, cc, r, n):
        wide_x = ref[cc, pl.ds(r, n + 16), :].astype(F32)
        return wide_x[16:], wide_x[15:-1], wide_x[14:-2]

    def conv(ref, cc, r, n, stream):
        x0, x1, x2 = shifts(ref, cc, r, n)
        return tap(stream, 0, cc) * x0 + tap(stream, 1, cc) * x1 + tap(stream, 2, cc) * x2

    def gate_block(cc, blk):
        h, i = blk // 4, blk % 4
        parts = []
        for e in range(2):
            r = pl.multiple_of((2 * h + e) * COLS + i * 128, 128)
            g = xo[cc, pl.ds(r, 128), :].astype(F32) * conv(xq, cc, r, 128, 0)
            parts.append(g.reshape(16, 8, CC))
        gs[cc, pl.ds(i * 16, 16), pl.ds(pl.multiple_of(h * 16, 16), 16), :] = jnp.concatenate(parts, 1).astype(BF16)

    def exchange(phase, src, dst, cc):
        def send(i):
            t = peer(i)
            remote(src.at[cc, t], dst.at[cc, s], a2a_s.at[phase, cc], a2a_r.at[phase, cc], (d, t)).start()

        loop(1, SEQ, send)
        local(src.at[cc, s], dst.at[cc, s], a2a_r.at[phase, cc]).start()

    def arrived(phase, dst, cc):
        wait_bytes(dst.at[cc], a2a_r.at[phase, cc])

    def halo_wait(n, cc):
        @pl.when(jnp.logical_not(last if n == 1 else first))
        def _():
            halo(n, cc).wait_recv()

    load(0, 0).wait()
    load(1, 0).wait()
    loop(0, 7, lambda n: gate_block(0, 7 - n))
    pl.semaphore_wait(barrier, DEVICES - 1)
    for n in (0, 2, 3):
        @pl.when(jnp.logical_not(last))
        def _():
            for cc in range(NC):
                halo(n, cc).start()

    @pl.when(jnp.logical_not(first))
    def _():
        for cc in range(NC):
            halo(1, cc).start()

    halo_wait(0, 0)
    gate_block(0, 0)
    exchange(0, gs, gr, 0)
    for cc in range(1, NC):
        load(0, cc).wait()
        load(1, cc).wait()
        halo_wait(0, cc)
        loop(0, 8, lambda n: gate_block(cc, n))
        exchange(0, gs, gr, cc)

    row = lax.broadcasted_iota(jnp.int32, (256, 256), 0)
    col = lax.broadcasted_iota(jnp.int32, (256, 256), 1)
    perm[...] = jnp.where(col == (row & 31) * 8 + (row >> 5), 1.0, 0.0).astype(BF16)
    perm_t[...] = jnp.where(row == (col & 31) * 8 + (col >> 5), 1.0, 0.0).astype(BF16)
    left_t[...] = jnp.transpose(left[...].astype(F32)).astype(BF16)
    right_t[...] = jnp.transpose(right[...].astype(F32)).astype(BF16)
    for a in range(ROWS):
        twist_t[a] = jnp.transpose(jnp.broadcast_to(twist[a : a + 1, :], (128, COLS)))
    twist_acc[...] = jnp.zeros_like(twist_acc)
    left_acc[...] = jnp.zeros_like(left_acc)
    right_acc[...] = jnp.zeros_like(right_acc)
    ckv[...] = jnp.zeros_like(ckv)
    cq[...] = jnp.zeros_like(cq)
    tws[...] = jnp.zeros_like(tws)

    def scaled(cc):
        def make_gated(blk):
            a, i = blk // 4, blk % 4
            r = pl.multiple_of(blk * 128, 128)
            gated[cc, a, pl.ds(pl.multiple_of(i * 128, 128), 128), :] = (
                conv(xk, cc, r, 128, 1) * conv(xv, cc, r, 128, 2)
            ).astype(BF16)

        loop(0, 16, make_gated)

        def mix(blk):
            h, i = blk // 2, blk % 2
            b = pl.ds(pl.multiple_of(i * 256, 256), 256)
            parts = []
            for e in range(2):
                m = dot(left[b, :], gated[cc, 2 * h + e]) * wide(twist_t[2 * h + e, b, :])
                parts.append(m.reshape(32, 8, CC))
            ss[cc, pl.ds(i * 32, 32), pl.ds(pl.multiple_of(h * 16, 16), 16), :] = jnp.concatenate(parts, 1).astype(BF16)

        loop(0, 4, mix)

    for cc in range(NC):
        for n in (2, 3):
            load(n, cc).wait()
            halo_wait(n, cc)
        scaled(cc)

    def spread(src, cc, put):
        def go(g):
            block = src[cc, pl.ds(g * 8, 8), :, :].reshape(256, CC)
            put(g, dot(perm[...], block).astype(BF16).reshape(8, 32, CC))

        loop(0, 8, go)

    def gather_back(dst, cc):
        def go(g):
            block = zb[:, pl.ds(pl.multiple_of(g * 32, 32), 32), :].reshape(256, CC)
            dst[cc, pl.ds(g * 8, 8), :, :] = dot(perm_t[...], block).astype(BF16).reshape(8, 32, CC)

        loop(0, 8, go)

    for cc in range(NC):
        arrived(0, gr, cc)

        def put_gd(g, value):
            gd[cc, :, pl.ds(pl.multiple_of(g * 32, 32), 32), :] = value

        spread(gr, cc, put_gd)

        def back_mul(b):
            zb[b] = dot(right_t[...], gd[cc, b]).astype(BF16)

        loop(0, 8, back_mul)
        gather_back(gr, cc)
        exchange(1, gr, br, cc)
    for cc in range(NC):
        exchange(2, ss, sr, cc)

    def after_rows(cc, stream, which):
        return remote(which.at[cc % 2, pl.ds(0, 8)], kh.at[cc, stream], kh_s.at[cc, stream], kh_r.at[cc, stream],
                      (d, jnp.maximum(s - 1, 0)))

    def kv_first(cc):
        par = cc % 2
        arrived(1, br, cc)

        def unpack(blk):
            h, i = blk // 4, blk % 4
            peers, half = pl.ds(i * 16, 16), pl.ds(pl.multiple_of(h * 16, 16), 16)
            b = pl.ds(pl.multiple_of(i * 128, 128), 128)
            grads, products = br[cc, peers, half, :].astype(F32), ss[cc, peers, half, :].astype(F32)
            for e in range(2):
                a = 2 * h + e
                g = grads[:, 8 * e : 8 * e + 8].reshape(128, CC)
                p = g * products[:, 8 * e : 8 * e + 8].reshape(128, CC)
                total = p[:, :128]
                for n in range(1, LANES):
                    total = total + p[:, n * 128 : (n + 1) * 128]
                twist_acc[a, b, :] += total
                mg[a, b, :] = (g * wide(twist_t[a, b, :])).astype(BF16)

        loop(0, 8, unpack)

        def left_terms(blk):
            a, i = blk // 2, blk % 2
            b = pl.ds(pl.multiple_of(i * 256, 256), 256)
            left_acc[b, :] += dot_nt(mg[a, b, :], gated[cc, a])

        loop(0, 8, left_terms)

        def back(blk):
            a, i = blk // 2, blk % 2
            r = pl.multiple_of(blk * 256, 256)
            g = dot(left_t[pl.ds(pl.multiple_of(i * 256, 256), 256), :], mg[a])
            gk[par, pl.ds(r, 256), :] = g * conv(xv, cc, r, 256, 2)
            gv[par, pl.ds(r, 256), :] = g * conv(xk, cc, r, 256, 1)

        loop(0, 8, back)

        @pl.when(jnp.logical_not(first))
        def _():
            after_rows(cc, 0, gk).start()
            after_rows(cc, 1, gv).start()

    def conv_back(grad, par, ref, cc, stream, total_ref, base):
        def step(blk, sums):
            r = pl.multiple_of(blk * 128, 128)
            g = grad[par, pl.ds(r, 136), :]
            obuf[stream, pl.ds(r, 128), :] = (
                tap(stream, 0, cc) * g[:128] + tap(stream, 1, cc) * g[1:129] + tap(stream, 2, cc) * g[2:130]
            ).astype(BF16)
            shifted = shifts(ref, cc, r, 128)
            return tuple(
                sums[j] + jnp.sum((g[:128] * shifted[j]).reshape(16, 8, CC), axis=0) for j in range(3)
            )

        sums = lax.fori_loop(0, 16, step, tuple(jnp.zeros((8, CC), F32) for _ in range(3)))
        for j in range(3):
            total = jnp.sum(sums[j], axis=0, keepdims=True)
            for n in range(LANES):
                total_ref[cc * LANES + n, base + j : base + j + 1, :] = total[:, n * 128 : (n + 1) * 128]

    outs = (q_out, k_out, v_out)

    def store(stream, cc):
        return local(obuf.at[stream], outs[stream].at[:, lane(cc)], out_sem.at[stream, cc])

    def finish(grad, par, ref, cc, stream, total_ref, base):
        if cc:
            store(stream, cc - 1).wait()
        conv_back(grad, par, ref, cc, stream, total_ref, base)
        store(stream, cc).start()

    def kv_second(cc):
        par = cc % 2

        @pl.when(jnp.logical_not(last))
        def _():
            after_rows(cc, 0, gk).wait_recv()
            after_rows(cc, 1, gv).wait_recv()

        @pl.when(jnp.logical_not(first))
        def _():
            after_rows(cc, 0, gk).wait_send()
            after_rows(cc, 1, gv).wait_send()

        gk[par, TOKENS : TOKENS + 8, :] = kh[cc, 0]
        gv[par, TOKENS : TOKENS + 8, :] = kh[cc, 1]
        finish(gk, par, xk, cc, 1, ckv, 0)
        finish(gv, par, xv, cc, 2, ckv, 3)

    def monarch(cc):
        arrived(2, sr, cc)

        def put_sd(g, value):
            sd[:, pl.ds(pl.multiple_of(g * 32, 32), 32), :] = value

        spread(sr, cc, put_sd)

        def mul(b):
            zb[b] = dot(right[...], sd[b]).astype(BF16)
            right_acc[...] += dot_nt(gd[cc, b], sd[b])

        loop(0, 8, mul)
        gather_back(sr, cc)

    def send_monarch(cc):
        exchange(3, sr, mr, cc)

        @pl.when(first)
        def _():
            def also(t):
                remote(sr.at[cc, t + 1, pl.ds(0, 16)], mh.at[cc], mh_s.at[cc], mh_r.at[cc], (d, t)).start()

            loop(1, SEQ - 1, also)
            local(sr.at[cc, 1, pl.ds(0, 16)], mh.at[cc], mh_r.at[cc]).start()

    partner = s + 1 - 2 * core

    def pair_copy():
        return remote(left_acc.at[pl.ds(pl.multiple_of((1 - core) * 256, 256), 256)], lx, l_s.at[0], l_r.at[0], (d, partner))

    def chip_of(i):
        t = (chip + i * 23) % 64
        return t, (t // 32, (t % 32) * 2 + core)

    def left_scatter():
        pair_copy().wait()
        half = left_acc[pl.ds(pl.multiple_of(core * 256, 256), 256), :] + lx[...]
        for n in range(4):
            lb[:, n] = half[:, n * 128 : (n + 1) * 128].astype(BF16).reshape(16, 16, 128)

        def send(i):
            t, dev = chip_of(i)
            remote(lb.at[t // 4, t % 4], li.at[chip], l_s.at[1], l_r.at[1], dev).start()

        loop(1, 64, send)
        local(lb.at[chip // 4, chip % 4], li.at[chip], l_r.at[1]).start()

    def left_gather():
        wait_bytes(li, l_r.at[1])
        lsum[...] = jnp.sum(li[...].astype(F32), axis=0).astype(BF16)

        def send(i):
            t, dev = chip_of(i)
            remote(lsum, lg.at[chip], l_s.at[2], l_r.at[2], dev).start()

        loop(1, 64, send)
        local(lsum, lg.at[chip], l_r.at[2]).start()

    def left_pair():
        return remote(lg, lg2, l_s.at[3], l_r.at[3], (d, partner))

    def left_finish():
        left_pair().wait()
        mine = lg[...].reshape(16, 4, 16, 128)
        other = lg2[...].reshape(16, 4, 16, 128)
        for n in range(4):
            left_out[pl.ds(pl.multiple_of(core * 256, 256), 256), n * 128 : (n + 1) * 128] = (
                mine[:, n].reshape(256, 128).astype(F32)
            )
            left_out[pl.ds(pl.multiple_of((1 - core) * 256, 256), 256), n * 128 : (n + 1) * 128] = (
                other[:, n].reshape(256, 128).astype(F32)
            )

    def to_owners(count, owner, src, inbox, ssem, rsem):
        def send(n):
            t = (n + me) % count
            dev = owner(t)

            @pl.when(dev == me)
            def _():
                local(src(t), inbox.at[me], rsem).start()

            @pl.when(dev != me)
            def _():
                remote(src(t), inbox.at[me], ssem, rsem, (dev // SEQ, dev % SEQ)).start()

        loop(0, count, send)

    def from_owner(count, owner, inbox, total, spread_to, rsem_in, ssem, rsem):
        def each(t):
            @pl.when(owner(t) == me)
            def _():
                wait_bytes(inbox, rsem_in)
                total[...] = jnp.sum(inbox[...].astype(F32), axis=0).astype(total.dtype)

                def send(i):
                    dev = (me + i * 37) % DEVICES
                    remote(total, spread_to.at[t], ssem, rsem, (dev // SEQ, dev % SEQ)).start()

                loop(1, DEVICES, send)
                local(total, spread_to.at[t], rsem).start()

        loop(0, count, each)

    def sent_to_owners(count, owner, src, ssem):
        def each(t):
            @pl.when(owner(t) != me)
            def _():
                wait_bytes(src.at[0], ssem)

        loop(0, count, each)

    def sent_by_owner(count, owner, inbox, ssem):
        def each(t):
            @pl.when(owner(t) == me)
            def _():
                wait_bytes(inbox.at[pl.ds(0, DEVICES - 1)], ssem)

        loop(0, count, each)

    def right_owner(t):
        n = t // 2
        return (t % 2) * SEQ + n * 4 + n % 4

    def kv_owner(t):
        return (t % 2) * SEQ + t * 10 + 3

    def q_owner(t):
        return ((t + 1) % 2) * SEQ + t * 10 + 8

    kv_first(0)
    kv_first(1)
    kv_second(0)
    kv_first(2)
    pair_copy().start()
    for a in range(ROWS):
        tws[a : a + 1, :] = jnp.sum(jnp.transpose(twist_acc[a]), axis=0, keepdims=True)
    twist_copy = remote(tws, twx, tw_s, tw_r, (1 - d, s))
    twist_copy.start()
    left_scatter()
    monarch(0)
    send_monarch(0)
    kv_second(1)
    monarch(1)
    send_monarch(1)
    kv_second(2)
    to_owners(TILES, kv_owner, lambda t: ckv.at[t], ci, c_s.at[0], c_r.at[0])
    left_gather()
    monarch(2)
    for n in range(2):
        rb[:, n] = right_acc[:, n * 128 : (n + 1) * 128].astype(BF16).reshape(16, 16, 128)
    to_owners(32, right_owner, lambda t: rb.at[t // 2, t % 2], ri, r_s.at[0], r_r.at[0])
    send_monarch(2)

    def query(cc):
        par = cc % 2
        arrived(3, mr, cc)

        @pl.when(jnp.logical_not(last))
        def _():
            wait_bytes(mh.at[cc], mh_r.at[cc])

        def unpack(blk):
            h, i = blk // 4, blk % 4
            m = mr[cc, pl.ds(i * 16, 16), pl.ds(pl.multiple_of(h * 16, 16), 16), :].astype(F32)
            for e in range(2):
                r = pl.multiple_of((2 * h + e) * COLS + i * 128, 128)
                gk[par, pl.ds(r, 128), :] = xo[cc, pl.ds(r, 128), :].astype(F32) * m[:, 8 * e : 8 * e + 8].reshape(128, CC)

        loop(0, 8, unpack)
        tail = xo[cc, TOKENS:WHOLE, :].astype(F32) * mh[cc].astype(F32)
        gk[par, TOKENS : TOKENS + 8, :] = tail[:8]
        finish(gk, par, xq, cc, 0, cq, 0)

    halo_wait(1, 0)
    query(0)
    from_owner(TILES, kv_owner, ci, csum.at[0], cg.at[0], c_r.at[0], c_s.at[1], c_r.at[1])
    halo_wait(1, 1)
    query(1)
    from_owner(32, right_owner, ri, rsum, rg, r_r.at[0], r_s.at[1], r_r.at[1])
    wait_bytes(lg, l_r.at[2])
    left_pair().start()
    twist_copy.wait()
    twist_out[...] = (tws[0:ROWS, :] + twx[0:ROWS, :]) / twist[...]
    halo_wait(1, 2)
    query(2)
    to_owners(TILES, q_owner, lambda t: cq.at[t], cj, c_s.at[2], c_r.at[2])
    left_finish()
    from_owner(TILES, q_owner, cj, csum.at[1], cg.at[1], c_r.at[2], c_s.at[3], c_r.at[3])
    wait_bytes(rg, r_r.at[1])
    for n in range(2):
        right_out[:, n * 128 : (n + 1) * 128] = (
            rg[...].reshape(16, 2, 16, 128)[:, n].reshape(256, 128).astype(F32)
        )
    wait_bytes(cg.at[0], c_r.at[1])
    wait_bytes(cg.at[1], c_r.at[3])
    for t in range(TILES):
        lanes = slice(t * 128, (t + 1) * 128)
        conv_out[0, :, lanes] = cg[1, t, 0:3, :]
        conv_out[1, :, lanes] = cg[0, t, 0:3, :]
        conv_out[2, :, lanes] = cg[0, t, 3:6, :]

    for stream in range(3):
        store(stream, NC - 1).wait()
    for phase, src in enumerate((gs, gr, ss, sr)):
        for cc in range(NC):
            wait_bytes(src.at[cc, pl.ds(0, SEQ - 1)], a2a_s.at[phase, cc])

    @pl.when(jnp.logical_not(last))
    def _():
        for n in (0, 2, 3):
            for cc in range(NC):
                halo(n, cc).wait_send()

    @pl.when(jnp.logical_not(first))
    def _():
        for cc in range(NC):
            halo(1, cc).wait_send()

    @pl.when(first)
    def _():
        for cc in range(NC):
            wait_bytes(sr.at[cc, pl.ds(0, SEQ - 2), pl.ds(0, 16)], mh_s.at[cc])

    wait_bytes(li.at[pl.ds(0, 63)], l_s.at[1])
    wait_bytes(li.at[pl.ds(0, 63)], l_s.at[2])
    sent_to_owners(32, right_owner, ri, r_s.at[0])
    sent_by_owner(32, right_owner, ri, r_s.at[1])
    sent_to_owners(TILES, kv_owner, ci, c_s.at[0])
    sent_by_owner(TILES, kv_owner, ci, c_s.at[1])
    sent_to_owners(TILES, q_owner, cj, c_s.at[2])
    sent_by_owner(TILES, q_owner, cj, c_s.at[3])


def vmem(*shape, dtype=BF16):
    return pltpu.VMEM(shape, dtype)


def dma(*shape):
    return pltpu.SemaphoreType.DMA(shape)


def shards(query_raw, key_raw, value_raw, out_grad, conv_taps, left_block, right_block, twiddle):
    flat = [a.reshape(TOKENS, CH) for a in (query_raw, key_raw, value_raw, out_grad)]
    anywhere, inside = pl.BlockSpec(memory_space=pl.ANY), pl.BlockSpec(memory_space=pltpu.VMEM)
    staged = vmem(NC, SEQ, 32, CC)
    scratch = (
        [vmem(NC, WHOLE, CC)] * 4
        + [staged] * 6
        + [vmem(NC, 8, 256, CC), vmem(NC, ROWS, COLS, CC), vmem(8, 256, CC), vmem(8, 256, CC), vmem(ROWS, COLS, CC)]
        + [vmem(2, TOKENS + 8, CC, dtype=F32)] * 2
        + [vmem(3, TOKENS, CC), vmem(NC, 16, CC), vmem(NC, 2, 8, CC, dtype=F32)]
        + [vmem(256, 256), vmem(256, 256), vmem(COLS, COLS), vmem(256, 256)]
        + [vmem(ROWS, COLS, 128, dtype=F32)] * 2
        + [vmem(8, COLS, dtype=F32)] * 2
        + [vmem(COLS, COLS, dtype=F32), vmem(256, 256, dtype=F32), vmem(256, COLS, dtype=F32)]
        + [vmem(16, 4, 16, 128), vmem(64, 16, 128), vmem(16, 128), vmem(64, 16, 128), vmem(64, 16, 128)]
        + [vmem(16, 2, 16, 128), vmem(DEVICES, 16, 128), vmem(16, 128), vmem(32, 16, 128)]
        + [vmem(TILES, 8, 128, dtype=F32)] * 2
        + [vmem(DEVICES, 8, 128, dtype=F32)] * 2
        + [vmem(2, 8, 128, dtype=F32), vmem(2, TILES, 8, 128, dtype=F32)]
        + [dma(4, NC), dma(4, NC), dma(4, NC), dma(4, NC), dma(4, NC), dma(NC), dma(NC), dma(NC, 2), dma(NC, 2), dma(3, NC)]
        + [dma(4), dma(4), dma(2), dma(2), dma(4), dma(4), dma(), dma()]
    )
    results = pl.pallas_call(
        kernel,
        name="monarch_back",
        out_shape=[
            jax.ShapeDtypeStruct((TOKENS, CH), BF16),
            jax.ShapeDtypeStruct((TOKENS, CH), BF16),
            jax.ShapeDtypeStruct((TOKENS, CH), BF16),
            jax.ShapeDtypeStruct((3, 3, CH), F32),
            jax.ShapeDtypeStruct((COLS, COLS), F32),
            jax.ShapeDtypeStruct((256, 256), F32),
            jax.ShapeDtypeStruct((ROWS, COLS), F32),
        ],
        in_specs=[anywhere] * 4 + [inside] * 4,
        out_specs=[anywhere] * 3 + [inside] * 4,
        scratch_shapes=scratch,
        compiler_params=pltpu.CompilerParams(
            collective_id=0, has_side_effects=True, vmem_limit_bytes=VMEM_LIMIT
        ),
    )(flat[0], flat[1], flat[2], flat[3], conv_taps, left_block, right_block, twiddle)
    return tuple(r.reshape(1, TOKENS, CH) for r in results[:3]) + tuple(results[3:])


def solution(mesh):
    rows = P("dp", "seq", None)
    return jax.shard_map(
        shards,
        mesh=mesh,
        in_specs=(rows, rows, rows, rows, P(), P(), P(), P("seq", None)),
        out_specs=(rows, rows, rows, P(), P(), P(), P("seq", None)),
        check_vma=False,
    )
```

time: 480 us -> 217 us (0.45)
  Pallas kernels: 0 us -> 204 us
  blocking collectives: 191 us -> 0 us
  waiting for transfers between devices: 88.3 us -> 0 us
  other arithmetic: 87.3 us -> 0 us
  local copies, waits for them, and re-layouts: 47.8 us -> 11.5 us
  starting transfers between devices: 28.1 us -> 0 us
  matrix products: 22.2 us -> 0 us
  between operations: 14.5 us -> 0.66 us
    pallas_call x0 -> x1, Pallas kernels: none -> 204 us  [shards(): pl.pallas_call(kernel, name='monarch_back', out_shape=[jax.ShapeDtypeStru...]
    all_to_all x2 -> x0, blocking collectives: 100 us -> none  [the longest x1 52.3 us: shards(): lax.all_to_all(gate_grad, 'seq', split_axis=2, concat_axis=1, tiled=True)]
    psum x2 -> x0, blocking collectives: 90.7 us -> none  [the longest x1 70.2 us: shards(): lax.psum((left_part, right_part, tap_part), ('dp', 'seq'))]
    psum x1 -> x0, waiting for transfers between devices: 57.6 us -> none  [shards(): lax.psum((left_part, right_part, tap_part), ('dp', 'seq'))]
    convert_element_type x12 -> x0, other arithmetic: 44.8 us -> none  [the longest x2 18.2 us: shards(): conv_back(grads[stream], after[stream], conv_taps[stream])]
    reduce_sum x3 -> x0, other arithmetic: 42.4 us -> none  [tap_terms(): jnp.sum(grads * padded[:, 1:-1], (0, 1))]
    convert_element_type x6 -> x0, local copies, waits for them, and re-layouts: 25.5 us -> none  [the longest x1 6.58 us: shards(): scaled_wide = scaled_grad.astype(jnp.float32)]
    dot_general x6 -> x0, matrix products: 22.2 us -> none  [the longest x1 5.64 us: shards(): jnp.einsum('nabc,nadc->bd', mixed_grad, gated, preferred_element_type=jnp...]
  transfers between devices with their start and end apart: 9 -> 0, of which waited for: 5 -> 0; matrix products, arithmetic and copies ran while one was open for 12% -> 0% of each run, Pallas kernels for 0% -> 0%
where the time goes in v1:
time: 217 us; the launch traced here: 216 us
  Pallas kernels  204 us (94%)
  local copies, waits for them, and re-layouts  11.5 us (5%)
    pallas_call x1, Pallas kernels, shards(): pl.pallas_call(kernel, name='monarch_back', out_shape=[jax.ShapeDtypeStru...  204 us
    unnamed x19, local copies, waits for them, and re-layouts  11.5 us

profile of v1, /device:TPU:1, one launch (start us, length us, event | category | flops | bytes accessed | tf_op | source)
XLA Modules:
  0.0 216.3 jit_solution(6223255371308992476)
XLA Ops:
  0.6 204.2 %monarch_back.1 = (bf16[2048,768]{1,0:T(8,128)(2,1)}, bf16[2048,768]{1,0:T(8,128)(2,1)}, bf16[2048,768]{1,0:T(8,128)(2,1)}, f32[3,3,768]{2,1,0:T(4,128)}, f32[51...) custom-call(bf16[2048,768]{1,0:T(8,128)(2,1)} %bitcast.10, bf16[2048,768]{1,0:T(8,128)(2,1)} %bitcast.11, ...), custom_call_target="tpu_custom_call" | custom-call | tf_op jit(solution)/shard_map/monarch_back/pallas_call | solution.py:610
  204.8 0.0 copy-start.1
  204.8 3.9 %copy.22 = bf16[1,2048,768]{2,1,0:T(8,128)(2,1)} copy(bf16[1,2048,768]{2,1,0:T(8,128)(2,1)} %bitcast.9) | data formatting | bytes 6291456
  208.7 0.0 copy-done.1
  208.7 0.0 copy-start
  208.7 1.7 copy.23
  210.4 1.4 copy-done
  211.8 0.0 copy-start.4
  211.8 0.0 copy-start.2
  211.8 0.0 copy-start.3
  211.8 0.0 copy-start.5
  211.8 1.7 copy.24
  213.4 0.0 copy-done.4
  213.4 0.6 copy.25
  214.1 0.0 copy-done.2
  214.1 1.0 copy.26
  215.0 0.0 copy-done.3
  215.0 0.7 copy.27
  215.7 0.0 copy-done.5
  215.7 0.6 copy.28
Async XLA Ops:
  204.8 3.9 %copy-start.1 = (bf16[2048,768]{1,0:T(8,128)(2,1)S(1)}, bf16[2048,768]{1,0:T(8,128)(2,1)}, u32[]{:S(2)}) copy-start(bf16[2048,768]{1,0:T(8,128)(2,1)} %get-tuple-element.15) | copy-start | bytes 9437188
  208.7 3.0 %copy-start = (bf16[2048,768]{1,0:T(8,128)(2,1)S(1)}, bf16[2048,768]{1,0:T(8,128)(2,1)}, u32[]{:S(2)}) copy-start(bf16[2048,768]{1,0:T(8,128)(2,1)} %get-tuple-element.16) | copy-start | bytes 9437188
  211.8 1.7 copy-start.4
  211.8 2.3 %copy-start.2 = (f32[512,512]{1,0:T(8,128)S(1)}, f32[512,512]{1,0:T(8,128)}, u32[]{:S(2)}) copy-start(f32[512,512]{1,0:T(8,128)} %get-tuple-element.32) | copy-start | bytes 3145732
  211.8 3.3 %copy-start.3 = (f32[256,256]{1,0:T(8,128)S(1)}, f32[256,256]{1,0:T(8,128)}, u32[]{:S(2)}) copy-start(f32[256,256]{1,0:T(8,128)} %get-tuple-element.33) | copy-start | bytes 786436
  211.8 4.0 %copy-start.5 = (f32[4,512]{1,0:T(4,128)S(1)}, f32[4,512]{1,0:T(4,128)}, u32[]{:S(2)}) copy-start(f32[4,512]{1,0:T(4,128)} %get-tuple-element.34) | copy-start | bytes 24580

commit v2 on v1

--- a/solution.py
+++ b/solution.py
@@ -44,10 +44,10 @@
     q_out, k_out, v_out, conv_out, left_out, right_out, twist_out,
     xq, xk, xv, xo, gs, gr, br, ss, sr, mr, gd, gated, sd, zb, mg, gk, gv,
     obuf, mh, kh, perm, perm_t, left_t, right_t, twist_t, twist_acc, tws, twx,
-    left_acc, right_acc, lx, lb, li, lsum, lg, lg2, rb, ri, rsum, rg,
-    ckv, cq, ci, cj, csum, cg,
+    left_acc, right_acc, lx, lb, li, lsum, lg, lg2, rx, kx, rb, ri, rsum, rg, rg2,
+    ckv, cq, cq_last, ia, ia_last, ib, ib_last, sb, sb_last,
     in_sem, halo_s, halo_r, a2a_s, a2a_r, mh_s, mh_r, kh_s, kh_r, out_sem,
-    l_s, l_r, r_s, r_r, c_s, c_r, tw_s, tw_r,
+    l_s, l_r, r_s, r_r, c_s, c_r, tw_s, tw_r, q_s, q_r,
 ):
     d, s = lax.axis_index("dp"), lax.axis_index("seq")
     x, zh, y, core = s // 16, (s // 8) % 2, (s // 2) % 4, s % 2
@@ -115,11 +115,11 @@
         mh[...] = jnp.zeros_like(mh)
         kh[...] = jnp.zeros_like(kh)
 
-    def tap(stream, j, cc):
-        return taps[stream, j : j + 1, cc * CC : (cc + 1) * CC]
-
-    def shifts(ref, cc, r, n):
-        wide_x = ref[cc, pl.ds(r, n + 16), :].astype(F32)
+    def tap(stream, j, cc, lo=0, hi=CC):
+        return taps[stream, j : j + 1, cc * CC + lo : cc * CC + hi]
+
+    def shifts(ref, cc, r, n, lo=0, hi=CC):
+        wide_x = ref[cc, pl.ds(r, n + 16), lo:hi].astype(F32)
         return wide_x[16:], wide_x[15:-1], wide_x[14:-2]
 
     def conv(ref, cc, r, n, stream):
@@ -135,16 +135,19 @@
             parts.append(g.reshape(16, 8, CC))
         gs[cc, pl.ds(i * 16, 16), pl.ds(pl.multiple_of(h * 16, 16), 16), :] = jnp.concatenate(parts, 1).astype(BF16)
 
-    def exchange(phase, src, dst, cc):
+    def exchange(phase, src, dst, cc, lanes=slice(None)):
+        def part(ref, t):
+            return ref.at[cc, t, :, lanes]
+
         def send(i):
             t = peer(i)
-            remote(src.at[cc, t], dst.at[cc, s], a2a_s.at[phase, cc], a2a_r.at[phase, cc], (d, t)).start()
+            remote(part(src, t), part(dst, s), a2a_s.at[phase, cc], a2a_r.at[phase, cc], (d, t)).start()
 
         loop(1, SEQ, send)
-        local(src.at[cc, s], dst.at[cc, s], a2a_r.at[phase, cc]).start()
-
-    def arrived(phase, dst, cc):
-        wait_bytes(dst.at[cc], a2a_r.at[phase, cc])
+        local(part(src, s), part(dst, s), a2a_r.at[phase, cc]).start()
+
+    def arrived(phase, dst, cc, lanes=slice(None)):
+        wait_bytes(dst.at[cc, :, :, lanes], a2a_r.at[phase, cc])
 
     def halo_wait(n, cc):
         @pl.when(jnp.logical_not(last if n == 1 else first))
@@ -189,7 +192,9 @@
     right_acc[...] = jnp.zeros_like(right_acc)
     ckv[...] = jnp.zeros_like(ckv)
     cq[...] = jnp.zeros_like(cq)
+    cq_last[...] = jnp.zeros_like(cq_last)
     tws[...] = jnp.zeros_like(tws)
+    rb[...] = jnp.zeros_like(rb)
 
     def scaled(cc):
         def make_gated(blk):
@@ -295,33 +300,54 @@
             after_rows(cc, 0, gk).start()
             after_rows(cc, 1, gv).start()
 
-    def conv_back(grad, par, ref, cc, stream, total_ref, base):
+    def conv_back(grad, par, ref, cc, stream, put, lo=0, hi=CC, write=True, count=True):
+        span = hi - lo
+
         def step(blk, sums):
             r = pl.multiple_of(blk * 128, 128)
-            g = grad[par, pl.ds(r, 136), :]
-            obuf[stream, pl.ds(r, 128), :] = (
-                tap(stream, 0, cc) * g[:128] + tap(stream, 1, cc) * g[1:129] + tap(stream, 2, cc) * g[2:130]
-            ).astype(BF16)
-            shifted = shifts(ref, cc, r, 128)
-            return tuple(
-                sums[j] + jnp.sum((g[:128] * shifted[j]).reshape(16, 8, CC), axis=0) for j in range(3)
-            )
-
-        sums = lax.fori_loop(0, 16, step, tuple(jnp.zeros((8, CC), F32) for _ in range(3)))
-        for j in range(3):
-            total = jnp.sum(sums[j], axis=0, keepdims=True)
-            for n in range(LANES):
-                total_ref[cc * LANES + n, base + j : base + j + 1, :] = total[:, n * 128 : (n + 1) * 128]
+            g = grad[par, pl.ds(r, 136), lo:hi]
+            if write:
+                obuf[stream, pl.ds(r, 128), lo:hi] = (
+                    tap(stream, 0, cc, lo, hi) * g[:128]
+                    + tap(stream, 1, cc, lo, hi) * g[1:129]
+                    + tap(stream, 2, cc, lo, hi) * g[2:130]
+                ).astype(BF16)
+            if count:
+                shifted = shifts(ref, cc, r, 128, lo, hi)
+                sums = tuple(sums[j] + jnp.sum((g[:128] * shifted[j]).reshape(16, 8, span), axis=0) for j in range(3))
+            return sums
+
+        sums = lax.fori_loop(0, 16, step, tuple(jnp.zeros((8, span), F32) for _ in range(3)))
+        if count:
+            for j in range(3):
+                total = jnp.sum(sums[j], axis=0, keepdims=True)
+                for n in range(span // 128):
+                    put(cc * LANES + lo // 128 + n, j, total[:, n * 128 : (n + 1) * 128])
 
     outs = (q_out, k_out, v_out)
 
-    def store(stream, cc):
-        return local(obuf.at[stream], outs[stream].at[:, lane(cc)], out_sem.at[stream, cc])
-
-    def finish(grad, par, ref, cc, stream, total_ref, base):
+    def store(stream, cc, half=None):
+        if half is None:
+            return local(obuf.at[stream], outs[stream].at[:, lane(cc)], out_sem.at[stream, cc])
+        return local(obuf.at[stream, :, pl.ds(half * 128, 128)], outs[stream].at[:, pl.ds(cc * CC + half * 128, 128)],
+                     out_sem.at[stream, cc + half])
+
+    def put_kv(base):
+        def put(tile, j, value):
+            ckv[tile, base + j : base + j + 1, :] = value
+
+        return put
+
+    def put_q(tile, j, value):
+        if tile == TILES - 1:
+            cq_last[j : j + 1, :] = value
+        else:
+            cq[3 * tile + j : 3 * tile + j + 1, :] = value
+
+    def finish(grad, par, ref, cc, stream, put):
         if cc:
             store(stream, cc - 1).wait()
-        conv_back(grad, par, ref, cc, stream, total_ref, base)
+        conv_back(grad, par, ref, cc, stream, put)
         store(stream, cc).start()
 
     def kv_second(cc):
@@ -339,8 +365,8 @@
 
         gk[par, TOKENS : TOKENS + 8, :] = kh[cc, 0]
         gv[par, TOKENS : TOKENS + 8, :] = kh[cc, 1]
-        finish(gk, par, xk, cc, 1, ckv, 0)
-        finish(gv, par, xv, cc, 2, ckv, 3)
+        finish(gk, par, xk, cc, 1, put_kv(0))
+        finish(gv, par, xv, cc, 2, put_kv(3))
 
     def monarch(cc):
         arrived(2, sr, cc)
@@ -357,8 +383,10 @@
         loop(0, 8, mul)
         gather_back(sr, cc)
 
+    low, high = pl.ds(0, 128), pl.ds(128, 128)
+
     def send_monarch(cc):
-        exchange(3, sr, mr, cc)
+        exchange(3, sr, mr, cc, low if cc == NC - 1 else slice(None))
 
         @pl.when(first)
         def _():
@@ -416,62 +444,77 @@
                 other[:, n].reshape(256, 128).astype(F32)
             )
 
-    def to_owners(count, owner, src, inbox, ssem, rsem):
-        def send(n):
-            t = (n + me) % count
-            dev = owner(t)
-
-            @pl.when(dev == me)
-            def _():
-                local(src(t), inbox.at[me], rsem).start()
-
-            @pl.when(dev != me)
-            def _():
-                remote(src(t), inbox.at[me], ssem, rsem, (dev // SEQ, dev % SEQ)).start()
-
-        loop(0, count, send)
-
-    def from_owner(count, owner, inbox, total, spread_to, rsem_in, ssem, rsem):
-        def each(t):
-            @pl.when(owner(t) == me)
-            def _():
-                wait_bytes(inbox, rsem_in)
-                total[...] = jnp.sum(inbox[...].astype(F32), axis=0).astype(total.dtype)
-
-                def send(i):
-                    dev = (me + i * 37) % DEVICES
-                    remote(total, spread_to.at[t], ssem, rsem, (dev // SEQ, dev % SEQ)).start()
-
-                loop(1, DEVICES, send)
-                local(total, spread_to.at[t], rsem).start()
-
-        loop(0, count, each)
-
-    def sent_to_owners(count, owner, src, ssem):
-        def each(t):
-            @pl.when(owner(t) != me)
-            def _():
-                wait_bytes(src.at[0], ssem)
-
-        loop(0, count, each)
-
-    def sent_by_owner(count, owner, inbox, ssem):
-        def each(t):
-            @pl.when(owner(t) == me)
-            def _():
-                wait_bytes(inbox.at[pl.ds(0, DEVICES - 1)], ssem)
-
-        loop(0, count, each)
-
-    def right_owner(t):
-        n = t // 2
-        return (t % 2) * SEQ + n * 4 + n % 4
-
-    def kv_owner(t):
-        return (t % 2) * SEQ + t * 10 + 3
-
-    def q_owner(t):
-        return ((t + 1) % 2) * SEQ + t * 10 + 8
+    def right_pair_copies():
+        return (
+            remote(right_acc.at[pl.ds(pl.multiple_of((1 - core) * 128, 128), 128)], rx, r_s.at[0], r_r.at[0], (d, partner)),
+            remote(ckv, kx, c_s, c_r, (d, partner)),
+        )
+
+    def right_scatter():
+        for copy in right_pair_copies():
+            copy.wait()
+        rx[...] += right_acc[pl.ds(pl.multiple_of(core * 128, 128), 128), :]
+        kx[...] += ckv[...]
+        for n in range(2):
+            for m in range(32):
+                rb[n * 32 + m, 0:4, :] = rx[m * 4 : m * 4 + 4, n * 128 : (n + 1) * 128]
+        for t in range(TILES):
+            for j in range(6):
+                rb[t * 6 + j, 4:5, :] = kx[t, j : j + 1, :]
+
+        def send(i):
+            t, dev = chip_of(i)
+            remote(rb.at[t], ri.at[chip], r_s.at[1], r_r.at[1], dev).start()
+
+        loop(1, 64, send)
+        local(rb.at[chip], ri.at[chip], r_r.at[1]).start()
+
+    def right_gather():
+        wait_bytes(ri, r_r.at[1])
+        rsum[...] = jnp.sum(ri[...], axis=0)
+
+        def send(i):
+            t, dev = chip_of(i)
+            remote(rsum, rg.at[chip], r_s.at[2], r_r.at[2], dev).start()
+
+        loop(1, 64, send)
+        local(rsum, rg.at[chip], r_r.at[2]).start()
+
+    def right_pair():
+        return remote(rg, rg2, r_s.at[3], r_r.at[3], (d, partner))
+
+    def right_finish():
+        right_pair().wait()
+        low_half, high_half = (
+            [jnp.where(core == n, rg[m, 0:4, :], rg2[m, 0:4, :]) for m in range(64)] for n in range(2)
+        )
+        for n in range(2):
+            for m in range(32):
+                right_out[m * 4 : m * 4 + 4, n * 128 : (n + 1) * 128] = low_half[n * 32 + m]
+                right_out[128 + m * 4 : 132 + m * 4, n * 128 : (n + 1) * 128] = high_half[n * 32 + m]
+
+    inner, outer = x * 2 + core, d * 8 + zh * 4 + y
+
+    def inner_dev(n):
+        return d, (((n // 2) * 2 + zh) * 4 + y) * 2 + n % 2
+
+    def outer_dev(n):
+        return n // 8, ((x * 2 + (n // 4) % 2) * 4 + n % 4) * 2 + core
+
+    def group_send(src, inbox, mine, n, dev_of, sem):
+        def send(i):
+            t = (mine + i) % n
+            remote(src, inbox.at[mine], q_s.at[sem], q_r.at[sem], dev_of(t)).start()
+
+        loop(1, n, send)
+        inbox[mine] = src[...]
+
+    def group_total(inbox, n, sem):
+        wait_bytes(inbox.at[pl.ds(0, n - 1)], q_r.at[sem])
+        return jnp.sum(inbox[...], axis=0)
+
+    def group_sent(inbox, n, sem):
+        wait_bytes(inbox.at[pl.ds(0, n - 1)], q_s.at[sem])
 
     kv_first(0)
     kv_first(1)
@@ -489,67 +532,92 @@
     monarch(1)
     send_monarch(1)
     kv_second(2)
-    to_owners(TILES, kv_owner, lambda t: ckv.at[t], ci, c_s.at[0], c_r.at[0])
+    monarch(2)
+    for copy in right_pair_copies():
+        copy.start()
+    send_monarch(2)
+    right_scatter()
     left_gather()
-    monarch(2)
-    for n in range(2):
-        rb[:, n] = right_acc[:, n * 128 : (n + 1) * 128].astype(BF16).reshape(16, 16, 128)
-    to_owners(32, right_owner, lambda t: rb.at[t // 2, t % 2], ri, r_s.at[0], r_r.at[0])
-    send_monarch(2)
-
-    def query(cc):
+
+    def query_first(cc, lo, hi):
         par = cc % 2
-        arrived(3, mr, cc)
+
+        def unpack(blk):
+            h, i = blk // 4, blk % 4
+            m = mr[cc, pl.ds(i * 16, 16), pl.ds(pl.multiple_of(h * 16, 16), 16), lo:hi].astype(F32)
+            for e in range(2):
+                r = pl.multiple_of((2 * h + e) * COLS + i * 128, 128)
+                gk[par, pl.ds(r, 128), lo:hi] = (
+                    xo[cc, pl.ds(r, 128), lo:hi].astype(F32) * m[:, 8 * e : 8 * e + 8].reshape(128, hi - lo)
+                )
+
+        loop(0, 8, unpack)
+        tail = xo[cc, TOKENS:WHOLE, lo:hi].astype(F32) * mh[cc, :, lo:hi].astype(F32)
+        gk[par, TOKENS : TOKENS + 8, lo:hi] = tail[:8]
+
+    def after_wait(cc):
+        halo_wait(1, cc)
 
         @pl.when(jnp.logical_not(last))
         def _():
             wait_bytes(mh.at[cc], mh_r.at[cc])
 
-        def unpack(blk):
-            h, i = blk // 4, blk % 4
-            m = mr[cc, pl.ds(i * 16, 16), pl.ds(pl.multiple_of(h * 16, 16), 16), :].astype(F32)
-            for e in range(2):
-                r = pl.multiple_of((2 * h + e) * COLS + i * 128, 128)
-                gk[par, pl.ds(r, 128), :] = xo[cc, pl.ds(r, 128), :].astype(F32) * m[:, 8 * e : 8 * e + 8].reshape(128, CC)
-
-        loop(0, 8, unpack)
-        tail = xo[cc, TOKENS:WHOLE, :].astype(F32) * mh[cc].astype(F32)
-        gk[par, TOKENS : TOKENS + 8, :] = tail[:8]
-        finish(gk, par, xq, cc, 0, cq, 0)
-
-    halo_wait(1, 0)
+    def query(cc):
+        arrived(3, mr, cc)
+        after_wait(cc)
+        query_first(cc, 0, CC)
+        finish(gk, cc % 2, xq, cc, 0, put_q)
+
+    END = NC - 1
+    exchange(4, sr, mr, END, high)
     query(0)
-    from_owner(TILES, kv_owner, ci, csum.at[0], cg.at[0], c_r.at[0], c_s.at[1], c_r.at[1])
-    halo_wait(1, 1)
     query(1)
-    from_owner(32, right_owner, ri, rsum, rg, r_r.at[0], r_s.at[1], r_r.at[1])
+    right_gather()
     wait_bytes(lg, l_r.at[2])
     left_pair().start()
     twist_copy.wait()
     twist_out[...] = (tws[0:ROWS, :] + twx[0:ROWS, :]) / twist[...]
-    halo_wait(1, 2)
-    query(2)
-    to_owners(TILES, q_owner, lambda t: cq.at[t], cj, c_s.at[2], c_r.at[2])
+    store(0, END - 1).wait()
+    arrived(3, mr, END, low)
+    after_wait(END)
+    query_first(END, 0, 128)
+    conv_back(gk, END % 2, xq, END, 0, put_q, 0, 128)
+    store(0, END, 0).start()
+    group_send(cq, ia, inner, 8, inner_dev, 0)
     left_finish()
-    from_owner(TILES, q_owner, cj, csum.at[1], cg.at[1], c_r.at[2], c_s.at[3], c_r.at[3])
-    wait_bytes(rg, r_r.at[1])
-    for n in range(2):
-        right_out[:, n * 128 : (n + 1) * 128] = (
-            rg[...].reshape(16, 2, 16, 128)[:, n].reshape(256, 128).astype(F32)
-        )
-    wait_bytes(cg.at[0], c_r.at[1])
-    wait_bytes(cg.at[1], c_r.at[3])
+    arrived(4, mr, END, high)
+    query_first(END, 128, 256)
+    conv_back(gk, END % 2, xq, END, 0, put_q, 128, 256, write=False)
+    group_send(cq_last, ia_last, inner, 8, inner_dev, 1)
+    sb[...] = group_total(ia, 8, 0)
+    group_send(sb, ib, outer, 16, outer_dev, 2)
+    conv_back(gk, END % 2, xq, END, 0, put_q, 128, 256, count=False)
+    wait_bytes(rg, r_r.at[2])
+    right_pair().start()
+    store(0, END, 1).start()
+    sb_last[...] = group_total(ia_last, 8, 1)
+    group_send(sb_last, ib_last, outer, 16, outer_dev, 3)
+    right_finish()
     for t in range(TILES):
         lanes = slice(t * 128, (t + 1) * 128)
-        conv_out[0, :, lanes] = cg[1, t, 0:3, :]
-        conv_out[1, :, lanes] = cg[0, t, 0:3, :]
-        conv_out[2, :, lanes] = cg[0, t, 3:6, :]
-
-    for stream in range(3):
-        store(stream, NC - 1).wait()
-    for phase, src in enumerate((gs, gr, ss, sr)):
-        for cc in range(NC):
-            wait_bytes(src.at[cc, pl.ds(0, SEQ - 1)], a2a_s.at[phase, cc])
+        for j in range(3):
+            conv_out[1, j : j + 1, lanes] = rg[t * 6 + j, 4:5, :]
+            conv_out[2, j : j + 1, lanes] = rg[t * 6 + 3 + j, 4:5, :]
+    total = group_total(ib, 16, 2)
+    for t in range(TILES - 1):
+        conv_out[0, :, t * 128 : (t + 1) * 128] = total[3 * t : 3 * t + 3, :]
+    conv_out[0, :, (TILES - 1) * 128 :] = group_total(ib_last, 16, 3)[0:3, :]
+
+    for stream in (1, 2):
+        store(stream, END).wait()
+    store(0, END, 0).wait()
+    store(0, END, 1).wait()
+    for phase, src in enumerate((gs, gr, ss, sr, sr)):
+        for cc in range(NC) if phase < 4 else (END,):
+            lanes = slice(None)
+            if phase >= 3 and cc == END:
+                lanes = low if phase == 3 else high
+            wait_bytes(src.at[cc, pl.ds(0, SEQ - 1), :, lanes], a2a_s.at[phase, cc])
 
     @pl.when(jnp.logical_not(last))
     def _():
@@ -569,12 +637,10 @@
 
     wait_bytes(li.at[pl.ds(0, 63)], l_s.at[1])
     wait_bytes(li.at[pl.ds(0, 63)], l_s.at[2])
-    sent_to_owners(32, right_owner, ri, r_s.at[0])
-    sent_by_owner(32, right_owner, ri, r_s.at[1])
-    sent_to_owners(TILES, kv_owner, ci, c_s.at[0])
-    sent_by_owner(TILES, kv_owner, ci, c_s.at[1])
-    sent_to_owners(TILES, q_owner, cj, c_s.at[2])
-    sent_by_owner(TILES, q_owner, cj, c_s.at[3])
+    wait_bytes(ri.at[pl.ds(0, 63)], r_s.at[1])
+    wait_bytes(ri.at[pl.ds(0, 63)], r_s.at[2])
+    for box, n, sem in ((ia, 8, 0), (ia_last, 8, 1), (ib, 16, 2), (ib_last, 16, 3)):
+        group_sent(box, n, sem)
 
 
 def vmem(*shape, dtype=BF16):
@@ -583,6 +649,25 @@
 
 def dma(*shape):
     return pltpu.SemaphoreType.DMA(shape)
+
+
+PIECES = 8
+
+
+def write_out(*refs):
+    ins, outs, through, (enter, leave) = refs[:7], refs[7:14], refs[14:21], refs[21:]
+    n_rows = TOKENS // PIECES
+    parts = [(n, p, pl.ds(p * n_rows, n_rows)) for p in range(PIECES) for n in range(3)]
+    parts += [(n, 0, slice(None)) for n in range(3, 7)]
+    first = [pltpu.make_async_copy(ins[n].at[r], through[n].at[r], enter.at[n, p]) for n, p, r in parts]
+    second = [pltpu.make_async_copy(through[n].at[r], outs[n].at[r], leave.at[n, p]) for n, p, r in parts]
+    for copy in first:
+        copy.start()
+    for copy, on in zip(first, second):
+        copy.wait()
+        on.start()
+    for copy in second:
+        copy.wait()
 
 
 def shards(query_raw, key_raw, value_raw, out_grad, conv_taps, left_block, right_block, twiddle):
@@ -600,12 +685,13 @@
         + [vmem(8, COLS, dtype=F32)] * 2
         + [vmem(COLS, COLS, dtype=F32), vmem(256, 256, dtype=F32), vmem(256, COLS, dtype=F32)]
         + [vmem(16, 4, 16, 128), vmem(64, 16, 128), vmem(16, 128), vmem(64, 16, 128), vmem(64, 16, 128)]
-        + [vmem(16, 2, 16, 128), vmem(DEVICES, 16, 128), vmem(16, 128), vmem(32, 16, 128)]
-        + [vmem(TILES, 8, 128, dtype=F32)] * 2
-        + [vmem(DEVICES, 8, 128, dtype=F32)] * 2
-        + [vmem(2, 8, 128, dtype=F32), vmem(2, TILES, 8, 128, dtype=F32)]
-        + [dma(4, NC), dma(4, NC), dma(4, NC), dma(4, NC), dma(4, NC), dma(NC), dma(NC), dma(NC, 2), dma(NC, 2), dma(3, NC)]
-        + [dma(4), dma(4), dma(2), dma(2), dma(4), dma(4), dma(), dma()]
+        + [vmem(128, 256, dtype=F32), vmem(TILES, 8, 128, dtype=F32), vmem(64, 8, 128, dtype=F32), vmem(64, 8, 128, dtype=F32)]
+        + [vmem(8, 128, dtype=F32), vmem(64, 8, 128, dtype=F32), vmem(64, 8, 128, dtype=F32)]
+        + [vmem(TILES, 8, 128, dtype=F32), vmem(16, 128, dtype=F32), vmem(8, 128, dtype=F32)]
+        + [vmem(8, 16, 128, dtype=F32), vmem(8, 8, 128, dtype=F32), vmem(16, 16, 128, dtype=F32), vmem(16, 8, 128, dtype=F32)]
+        + [vmem(16, 128, dtype=F32), vmem(8, 128, dtype=F32)]
+        + [dma(4, NC), dma(4, NC), dma(4, NC), dma(5, NC), dma(5, NC), dma(NC), dma(NC), dma(NC, 2), dma(NC, 2), dma(3, NC + 1)]
+        + [dma(4), dma(4), dma(4), dma(4), dma(), dma(), dma(), dma(), dma(4), dma(4)]
     )
     results = pl.pallas_call(
         kernel,
@@ -626,6 +712,15 @@
             collective_id=0, has_side_effects=True, vmem_limit_bytes=VMEM_LIMIT
         ),
     )(flat[0], flat[1], flat[2], flat[3], conv_taps, left_block, right_block, twiddle)
+    results = pl.pallas_call(
+        write_out,
+        name="write_out",
+        out_shape=[jax.ShapeDtypeStruct(r.shape, r.dtype) for r in results],
+        in_specs=[pl.BlockSpec(memory_space=pltpu.HBM)] * 7,
+        out_specs=[pl.BlockSpec(memory_space=pltpu.HBM)] * 7,
+        scratch_shapes=[pltpu.VMEM(r.shape, r.dtype) for r in results] + [dma(7, PIECES)] * 2,
+        compiler_params=pltpu.CompilerParams(vmem_limit_bytes=VMEM_LIMIT),
+    )(*results)
     return tuple(r.reshape(1, TOKENS, CH) for r in results[:3]) + tuple(results[3:])
 
 

time: 217 us -> 208 us (0.959)
  local copies, waits for them, and re-layouts: 11.5 us -> 0 us
  Pallas kernels: 204 us -> 208 us
    unnamed x19 -> x0, local copies, waits for them, and re-layouts: 11.5 us -> none
    pallas_call x0 -> x1, Pallas kernels: none -> 9.04 us  [shards(): pl.pallas_call(write_out, name='write_out', out_shape=[jax.ShapeDtypeStru...]
    pallas_call x1, Pallas kernels: 204 us -> 199 us  [shards(): pl.pallas_call(kernel, name='monarch_back', out_shape=[jax.ShapeDtypeStru...]
where the time goes in v2:
time: 208 us
  Pallas kernels  208 us (100%)
    pallas_call x1, Pallas kernels, shards(): pl.pallas_call(kernel, name='monarch_back', out_shape=[jax.ShapeDtypeStru...  199 us
    pallas_call x1, Pallas kernels, shards(): pl.pallas_call(write_out, name='write_out', out_shape=[jax.ShapeDtypeStru...  9.04 us

profile of v2, /device:TPU:1, one launch (start us, length us, event | category | flops | bytes accessed | tf_op | source)
XLA Modules:
  0.0 208.2 jit_solution(5988435292657150639)
XLA Ops:
  0.6 198.6 %monarch_back.1 = (bf16[2048,768]{1,0:T(8,128)(2,1)}, bf16[2048,768]{1,0:T(8,128)(2,1)}, bf16[2048,768]{1,0:T(8,128)(2,1)}, f32[3,3,768]{2,1,0:T(4,128)}, f32[51...) custom-call(bf16[2048,768]{1,0:T(8,128)(2,1)} %bitcast.7, bf16[2048,768]{1,0:T(8,128)(2,1)} %bitcast.8, ...), custom_call_target="tpu_custom_call" | custom-call | tf_op jit(solution)/shard_map/monarch_back/pallas_call | solution.py:696
  199.2 9.0 %write_out.1 = (bf16[2048,768]{1,0:T(8,128)(2,1)}, bf16[2048,768]{1,0:T(8,128)(2,1)}, bf16[2048,768]{1,0:T(8,128)(2,1)}, f32[3,3,768]{2,1,0:T(4,128)}, f32[512,5...) custom-call(bf16[2048,768]{1,0:T(8,128)(2,1)} %get-tuple-element.21.refs_0_, ...), custom_call_target="tpu_custom_call" | custom-call | tf_op jit(solution)/shard_map/write_out/pallas_call | solution.py:715

commit v3 on v2

--- a/solution.py
+++ b/solution.py
@@ -651,14 +651,14 @@
     return pltpu.SemaphoreType.DMA(shape)
 
 
-PIECES = 8
+PIECES = 16
 
 
 def write_out(*refs):
     ins, outs, through, (enter, leave) = refs[:7], refs[7:14], refs[14:21], refs[21:]
     n_rows = TOKENS // PIECES
-    parts = [(n, p, pl.ds(p * n_rows, n_rows)) for p in range(PIECES) for n in range(3)]
-    parts += [(n, 0, slice(None)) for n in range(3, 7)]
+    parts = [(n, 0, slice(None)) for n in range(3, 7)]
+    parts += [(n, p, pl.ds(p * n_rows, n_rows)) for p in range(PIECES) for n in range(3)]
     first = [pltpu.make_async_copy(ins[n].at[r], through[n].at[r], enter.at[n, p]) for n, p, r in parts]
     second = [pltpu.make_async_copy(through[n].at[r], outs[n].at[r], leave.at[n, p]) for n, p, r in parts]
     for copy in first:

time: 208 us -> 209 us (level)
  no operation moved by 1% of the time
where the time goes in v3:
time: 209 us
  Pallas kernels  209 us (100%)
    pallas_call x1, Pallas kernels, shards(): pl.pallas_call(kernel, name='monarch_back', out_shape=[jax.ShapeDtypeStru...  199 us
    pallas_call x1, Pallas kernels, shards(): pl.pallas_call(write_out, name='write_out', out_shape=[jax.ShapeDtypeStru...  9.98 us

profile of v3, /device:TPU:1, one launch (start us, length us, event | category | flops | bytes accessed | tf_op | source)
XLA Modules:
  0.0 209.2 jit_solution(16807939105029997316)
XLA Ops:
  0.6 198.6 %monarch_back.1 = (bf16[2048,768]{1,0:T(8,128)(2,1)}, bf16[2048,768]{1,0:T(8,128)(2,1)}, bf16[2048,768]{1,0:T(8,128)(2,1)}, f32[3,3,768]{2,1,0:T(4,128)}, f32[51...) custom-call(bf16[2048,768]{1,0:T(8,128)(2,1)} %bitcast.7, bf16[2048,768]{1,0:T(8,128)(2,1)} %bitcast.8, ...), custom_call_target="tpu_custom_call" | custom-call | tf_op jit(solution)/shard_map/monarch_back/pallas_call | solution.py:696
  199.2 10.0 %write_out.1 = (bf16[2048,768]{1,0:T(8,128)(2,1)}, bf16[2048,768]{1,0:T(8,128)(2,1)}, bf16[2048,768]{1,0:T(8,128)(2,1)}, f32[3,3,768]{2,1,0:T(4,128)}, f32[512,5...) custom-call(bf16[2048,768]{1,0:T(8,128)(2,1)} %get-tuple-element.21.refs_0_, ...), custom_call_target="tpu_custom_call" | custom-call | tf_op jit(solution)/shard_map/write_out/pallas_call | solution.py:715
